TPU v7x, 32 devices: a whole 2x2x4 slice. The times are simulated.
32 devices in a mesh: dp: 8 (over y, x, core), mp: 4 (over z).
Axes of the slice: x: 2, y: 2, z: 4, core: 2. Of those that a mesh axis runs over, the one named last changes fastest.
Arguments:
- hidden_in: bfloat16 [16, 1024, 768], P('dp', 'mp'), may hold values from -6 to 6
- out_grad: bfloat16 [16, 1024, 768], P('dp', 'mp'), may hold values from -6 to 6
- seg_ids: int32 [16, 1024], P('dp'), may hold values from 0 to 3, as said below
- row_len: int32 [16], P('dp'), may hold values from 512 to 1024
- slot_mask: int32 [16, 16], P('dp'), may hold values 0 or 1
- mem_keys: bfloat16 [16, 32, 768], P('dp', None, 'mp'), may hold values from -6 to 6
- mem_values: bfloat16 [16, 32, 768], P('dp', None, 'mp'), may hold values from -6 to 6
- w_qkv: float32 [3, 768, 768], P(None, 'dp', 'mp'), may hold values from -0.21875 to 0.21875
- m_qkv: float32 [3, 768, 768], P(None, 'dp', 'mp'), as said below
- v_qkv: float32 [3, 768, 768], P(None, 'dp', 'mp'), may hold values from 8192 to 131072, as said below
- w_attn_out: float32 [768, 768], P('mp', 'dp'), may hold values from -1.25 to 1.25
- m_attn_out: float32 [768, 768], P('mp', 'dp'), as said below
- v_attn_out: float32 [768, 768], P('mp', 'dp'), may hold values from 512 to 8192, as said below
- w_up: float32 [768, 3072], P('dp', 'mp'), may hold values from -0.21875 to 0.21875
- m_up: float32 [768, 3072], P('dp', 'mp'), as said below
- v_up: float32 [768, 3072], P('dp', 'mp'), may hold values from 512 to 8192, as said below
- w_down: float32 [3072, 768], P('mp', 'dp'), may hold values from -0.109375 to 0.109375
- m_down: float32 [3072, 768], P('mp', 'dp'), as said below
- v_down: float32 [3072, 768], P('mp', 'dp'), may hold values from 2048 to 32768, as said below
- gains: float32 [2, 768], replicated, may hold values from 0.5 to 1.5
- m_gains: float32 [2, 768], replicated, as said below
- v_gains: float32 [2, 768], replicated, may hold values from 8192 to 131072, as said below
- rel_table: float32 [32, 12], replicated, may hold values from -4 to 4
- m_rel: float32 [32, 12], replicated, as said below
- v_rel: float32 [32, 12], replicated, may hold values from 8192 to 131072, as said below
Outputs:
- output: bfloat16 [16, 1024, 768], P('dp', 'mp')
- grad_input: float32 [16, 1024, 768], P('dp', 'mp')
- qkv_new: float32 [3, 768, 768], P(None, 'dp', 'mp')
- qkv_first: float32 [3, 768, 768], P(None, 'dp', 'mp')
- qkv_second: float32 [3, 768, 768], P(None, 'dp', 'mp')
- qkv_copy: bfloat16 [3, 768, 768], P(None, 'dp', 'mp')
- attn_out_new: float32 [768, 768], P('mp', 'dp')
- attn_out_first: float32 [768, 768], P('mp', 'dp')
- attn_out_second: float32 [768, 768], P('mp', 'dp')
- attn_out_copy: bfloat16 [768, 768], P('mp', 'dp')
- up_new: float32 [768, 3072], P('dp', 'mp')
- up_first: float32 [768, 3072], P('dp', 'mp')
- up_second: float32 [768, 3072], P('dp', 'mp')
- up_copy: bfloat16 [768, 3072], P('dp', 'mp')
- down_new: float32 [3072, 768], P('mp', 'dp')
- down_first: float32 [3072, 768], P('mp', 'dp')
- down_second: float32 [3072, 768], P('mp', 'dp')
- down_copy: bfloat16 [3072, 768], P('mp', 'dp')
- gains_new: float32 [2, 768], replicated
- gains_first: float32 [2, 768], replicated
- gains_second: float32 [2, 768], replicated
- rel_new: float32 [32, 12], replicated
- rel_first: float32 [32, 12], replicated
- rel_second: float32 [32, 12], replicated
Inputs may be any that keep to these rules, and one draw needn't show every extreme that they name: `seg_ids`: in every row the document numbers start at 0 and never fall; in each aligned block of 2 rows one row, drawn from the seed, is a single document with row_len 1024. `m_qkv`: both signs. `v_qkv`: positive. `m_attn_out`: both signs. `v_attn_out`: positive. `m_up`: both signs. `v_up`: positive. `m_down`: both signs. `v_down`: positive. `m_gains`: both signs. `v_gains`: positive. `m_rel`: both signs. `v_rel`: positive.
All inputs are finite; a program needn't handle non-finite values. No bound on the sum of `slot_mask` on one device may be relied on, other than what follows from the above.
Results may differ from a plain program's by a relative error of at most 0.017.
Values may be sent and summed in bfloat16 or wider, within the bound.
A program may use at most 256 MiB of HBM per device.

v0:
```python
import jax
import jax.numpy as jnp
from jax import lax
from jax.sharding import PartitionSpec as P

HEAD_DIM = 64
STEP = 10


NORM_EPS = 1e-06
MOMENT_DECAY = 0.5
ADAM_EPS = 1e-08
MATRIX_RATE = 0.05
SMALL_RATE = 0.5
WEIGHT_DECAY = 0.01
FAR_BOUNDS = (12, 16, 23, 32, 46, 64, 91)
NEG_FILL = -1e30


def bucket_of(distance):
    far_dist = jnp.abs(distance)
    far_bucket = jnp.full(far_dist.shape, 8, jnp.int32)
    for far_bound in FAR_BOUNDS:
        far_bucket = far_bucket + (far_dist >= far_bound).astype(jnp.int32)
    one_side = jnp.where(far_dist < 8, far_dist, far_bucket)
    return one_side + jnp.where(distance > 0, 16, 0).astype(jnp.int32)


def gelu_exact(values):
    return jax.nn.gelu(values, approximate=False)


def rms_inverse(values):
    return lax.rsqrt(jnp.mean(values * values, axis=-1, keepdims=True) + NORM_EPS)


def norm_back(grad_out, normed_hat, inverse, gain_row):
    scaled = grad_out * gain_row
    return inverse * (scaled - normed_hat * jnp.mean(scaled * normed_hat, axis=-1, keepdims=True))


def adamw(weight, gradient, first_mom, second, step_rate, decay_rate):
    first_new = MOMENT_DECAY * first_mom + (1.0 - MOMENT_DECAY) * gradient
    second_new = MOMENT_DECAY * second + (1.0 - MOMENT_DECAY) * gradient * gradient
    bias_fix = 1.0 - MOMENT_DECAY**STEP
    update = first_new / bias_fix / (jnp.sqrt(second_new / bias_fix) + ADAM_EPS)
    return (weight - step_rate * (update + decay_rate * weight), first_new, second_new)


def row_masks(seg_row, length, pair_on):
    positions = jnp.arange(seg_row.shape[0], dtype=jnp.int32)
    is_live = positions < length
    doc_group = jnp.where(is_live, seg_row, -1).astype(jnp.int32)
    slot_on = jnp.repeat(pair_on, 2) > 0
    return (is_live[:, None] & slot_on[None, :], doc_group[:, None] == doc_group[None, :])


def block_scores(q_block, mk_row, k_row, mem_ok, tok_ok, bias_block, score_scale):
    mem_raw = (
        jnp.einsum("hqe,hke->hqk", q_block, mk_row, preferred_element_type=jnp.float32)
        * score_scale
    )
    tok_raw = (
        jnp.einsum("hqe,hke->hqk", q_block, k_row, preferred_element_type=jnp.float32) * score_scale
        + bias_block
    )
    return (jnp.where(mem_ok[None], mem_raw, NEG_FILL), jnp.where(tok_ok[None], tok_raw, NEG_FILL))


def on_device(
    hidden_in,
    out_grad,
    seg_ids,
    row_len,
    slot_mask,
    mem_keys,
    mem_values,
    w_qkv,
    m_qkv,
    v_qkv,
    w_attn_out,
    m_attn_out,
    v_attn_out,
    w_up,
    m_up,
    v_up,
    w_down,
    m_down,
    v_down,
    gains,
    m_gains,
    v_gains,
    rel_table,
    m_rel,
    v_rel,
):
    qkv_low, attn_out_low, up_low, down_low = (
        lax.all_gather(w_qkv.astype(jnp.bfloat16), "dp", axis=1, tiled=True),
        lax.all_gather(w_attn_out.astype(jnp.bfloat16), "dp", axis=1, tiled=True),
        lax.all_gather(w_up.astype(jnp.bfloat16), "dp", axis=0, tiled=True),
        lax.all_gather(w_down.astype(jnp.bfloat16), "dp", axis=1, tiled=True),
    )
    row_count = hidden_in.shape[0]
    seq_span = seg_ids.shape[1]
    bucket_total, head_total = rel_table.shape
    head_local = head_total // lax.axis_size("mp")
    head_size = HEAD_DIM
    model_width = gains.shape[1]
    slots = mem_keys.shape[1]
    score_scale = head_size ** (-0.5)
    block_rows = min(512, seq_span)
    mp_index = lax.axis_index("mp")
    positions = jnp.arange(seq_span, dtype=jnp.int32)
    bucket_grid = bucket_of(positions[None, :] - positions[:, None])
    table_local = lax.dynamic_slice_in_dim(rel_table, mp_index * head_local, head_local, 1)
    rel_bias = jnp.zeros((head_local, seq_span, seq_span), jnp.float32)
    for bucket_number in range(bucket_total):
        rel_bias = rel_bias + jnp.where(
            (bucket_grid == bucket_number)[None], table_local[bucket_number][:, None, None], 0.0
        )
    qkv_heads = qkv_low.reshape(3, model_width, head_local, head_size)
    attn_out_heads = attn_out_low.reshape(head_local, head_size, model_width)
    inputs = hidden_in.astype(jnp.float32)
    inverse_one = rms_inverse(inputs)
    hat_one = inputs * inverse_one
    normed_one = (hat_one * gains[0]).astype(jnp.bfloat16)
    normed_full = lax.all_gather(normed_one, "mp", axis=1, tiled=True)
    project = jnp.einsum(
        "rsd,cdhe->crhse", normed_full, qkv_heads, preferred_element_type=jnp.float32
    ).astype(jnp.bfloat16)
    queries, key_new, value_new = (project[0], project[1], project[2])
    mem_key_rows = jnp.transpose(
        mem_keys.reshape(row_count, slots, head_local, head_size), (0, 2, 1, 3)
    )
    mem_value_rows = jnp.transpose(
        mem_values.reshape(row_count, slots, head_local, head_size), (0, 2, 1, 3)
    )

    def forward_row(packed):
        q_row, k_row, v_row, mk_row, mv_row, seg_row, length, pair_on = packed
        mem_allowed, tok_allowed = row_masks(seg_row, length, pair_on)
        contexts = []
        maxima = []
        for first_row in range(0, seq_span, block_rows):
            last_row = first_row + block_rows
            mem_s, tok_s = block_scores(
                q_row[:, first_row:last_row],
                mk_row,
                k_row,
                mem_allowed[first_row:last_row],
                tok_allowed[first_row:last_row],
                rel_bias[:, first_row:last_row],
                score_scale,
            )
            row_peak = jnp.maximum(
                jnp.max(mem_s, axis=-1, keepdims=True), jnp.max(tok_s, axis=-1, keepdims=True)
            )
            mem_exp = jnp.exp(mem_s - row_peak)
            tok_exp = jnp.exp(tok_s - row_peak)
            exp_total = jnp.sum(mem_exp, axis=-1, keepdims=True) + jnp.sum(
                tok_exp, axis=-1, keepdims=True
            )
            mem_prob = (mem_exp / exp_total).astype(jnp.bfloat16)
            tok_prob = (tok_exp / exp_total).astype(jnp.bfloat16)
            block_context = jnp.einsum(
                "hqk,hke->hqe", mem_prob, mv_row, preferred_element_type=jnp.float32
            )
            block_context = block_context + jnp.einsum(
                "hqk,hke->hqe", tok_prob, v_row, preferred_element_type=jnp.float32
            )
            contexts.append(block_context.astype(jnp.bfloat16))
            maxima.append((row_peak + jnp.log(exp_total))[:, :, 0])
        return (jnp.concatenate(contexts, axis=1), jnp.concatenate(maxima, axis=1))

    context, log_totals = lax.map(
        forward_row,
        (queries, key_new, value_new, mem_key_rows, mem_value_rows, seg_ids, row_len, slot_mask),
    )
    attn_term = jnp.einsum(
        "rhse,hed->rsd", context, attn_out_heads, preferred_element_type=jnp.float32
    )
    attn_local = lax.psum_scatter(attn_term, "mp", scatter_dimension=1, tiled=True)
    mid = inputs + attn_local
    inverse_two = rms_inverse(mid)
    hat_two = mid * inverse_two
    normed_two = (hat_two * gains[1]).astype(jnp.bfloat16)
    ffn_source = lax.all_gather(normed_two, "mp", axis=1, tiled=True)
    up_full, down_full = (up_low, down_low)
    pre_act = jnp.einsum("rsd,df->rsf", ffn_source, up_full, preferred_element_type=jnp.float32)
    act_value, act_back = jax.vjp(gelu_exact, pre_act)
    act_low = act_value.astype(jnp.bfloat16)
    ffn_term = jnp.einsum("rsf,fd->rsd", act_low, down_full, preferred_element_type=jnp.float32)
    ffn_local = lax.psum_scatter(
        ffn_term.astype(jnp.bfloat16), "mp", scatter_dimension=1, tiled=True
    ).astype(jnp.float32)
    output = (mid + ffn_local).astype(jnp.bfloat16)
    grad_top = out_grad.astype(jnp.float32)
    grad_source = lax.all_gather(out_grad, "mp", axis=1, tiled=True)
    down_grad = jnp.einsum("rsf,rsd->fd", act_low, grad_source, preferred_element_type=jnp.float32)
    grad_act = jnp.einsum("rsd,fd->rsf", grad_source, down_full, preferred_element_type=jnp.float32)
    grad_pre = act_back(grad_act)[0].astype(jnp.bfloat16)
    up_grad = jnp.einsum("rsd,rsf->df", ffn_source, grad_pre, preferred_element_type=jnp.float32)
    grad_normed_part = jnp.einsum(
        "rsf,df->rsd", grad_pre, up_full, preferred_element_type=jnp.float32
    )
    grad_normed_two = lax.psum_scatter(grad_normed_part, "mp", scatter_dimension=1, tiled=True)
    gain_two_grad = jnp.sum(grad_normed_two * hat_two, axis=(0, 1))
    grad_mid = grad_top + norm_back(grad_normed_two, hat_two, inverse_two, gains[1])
    grad_mid_low = grad_mid.astype(jnp.bfloat16)
    grad_attn_full = lax.all_gather(grad_mid_low, "mp", axis=1, tiled=True)
    attn_out_grad = jnp.einsum(
        "rhse,rsd->hed", context, grad_attn_full, preferred_element_type=jnp.float32
    )
    attn_out_grad = attn_out_grad.reshape(head_local * head_size, model_width)
    grad_context = jnp.einsum(
        "rsd,hed->rhse", grad_attn_full, attn_out_heads, preferred_element_type=jnp.float32
    ).astype(jnp.bfloat16)

    def backward_row(bias_total, packed):
        q_row, k_row, v_row, mk_row, mv_row, seg_row, length, pair_on, lse_row, grad_row = packed
        mem_allowed, tok_allowed = row_masks(seg_row, length, pair_on)
        key_acc = jnp.zeros(k_row.shape, jnp.float32)
        value_acc = jnp.zeros(v_row.shape, jnp.float32)
        query_parts = []
        bias_parts = []
        for first_row in range(0, seq_span, block_rows):
            last_row = first_row + block_rows
            q_block = q_row[:, first_row:last_row]
            mem_s, tok_s = block_scores(
                q_block,
                mk_row,
                k_row,
                mem_allowed[first_row:last_row],
                tok_allowed[first_row:last_row],
                rel_bias[:, first_row:last_row],
                score_scale,
            )
            lse_block = lse_row[:, first_row:last_row, None]
            mem_prob = jnp.exp(mem_s - lse_block)
            tok_prob = jnp.exp(tok_s - lse_block)
            grad_block = grad_row[:, first_row:last_row]
            mem_gprob = jnp.einsum(
                "hqe,hke->hqk", grad_block, mv_row, preferred_element_type=jnp.float32
            )
            tok_gprob = jnp.einsum(
                "hqe,hke->hqk", grad_block, v_row, preferred_element_type=jnp.float32
            )
            row_dot = jnp.sum(mem_prob * mem_gprob, axis=-1, keepdims=True) + jnp.sum(
                tok_prob * tok_gprob, axis=-1, keepdims=True
            )
            mem_gscore = (mem_prob * (mem_gprob - row_dot)).astype(jnp.bfloat16)
            tok_gscore = (tok_prob * (tok_gprob - row_dot)).astype(jnp.bfloat16)
            query_grad = jnp.einsum(
                "hqk,hke->hqe", mem_gscore, mk_row, preferred_element_type=jnp.float32
            )
            query_grad = query_grad + jnp.einsum(
                "hqk,hke->hqe", tok_gscore, k_row, preferred_element_type=jnp.float32
            )
            query_parts.append((query_grad * score_scale).astype(jnp.bfloat16))
            key_acc = key_acc + jnp.einsum(
                "hqk,hqe->hke", tok_gscore, q_block, preferred_element_type=jnp.float32
            )
            value_acc = value_acc + jnp.einsum(
                "hqk,hqe->hke",
                tok_prob.astype(jnp.bfloat16),
                grad_block,
                preferred_element_type=jnp.float32,
            )
            bias_parts.append(tok_gscore.astype(jnp.float32))
        bias_total = bias_total + jnp.concatenate(bias_parts, axis=1)
        row_grads = (
            jnp.concatenate(query_parts, axis=1),
            (key_acc * score_scale).astype(jnp.bfloat16),
            value_acc.astype(jnp.bfloat16),
        )
        return (bias_total, row_grads)

    bias_grad, (grad_q, grad_k, grad_v) = lax.scan(
        backward_row,
        jnp.zeros((head_local, seq_span, seq_span), jnp.float32),
        (
            queries,
            key_new,
            value_new,
            mem_key_rows,
            mem_value_rows,
            seg_ids,
            row_len,
            slot_mask,
            log_totals,
            grad_context,
        ),
    )
    grad_project = jnp.stack([grad_q, grad_k, grad_v])
    qkv_grad = jnp.einsum(
        "rsd,crhse->cdhe", normed_full, grad_project, preferred_element_type=jnp.float32
    )
    qkv_grad = qkv_grad.reshape(3, model_width, head_local * head_size)
    grad_normed_term = jnp.einsum(
        "crhse,cdhe->rsd", grad_project, qkv_heads, preferred_element_type=jnp.float32
    )
    grad_normed_one = lax.psum_scatter(
        grad_normed_term.astype(jnp.bfloat16), "mp", scatter_dimension=1, tiled=True
    ).astype(jnp.float32)
    gain_one_grad = jnp.sum(grad_normed_one * hat_one, axis=(0, 1))
    grad_input = grad_mid + norm_back(grad_normed_one, hat_one, inverse_one, gains[0])
    bucket_sums = []
    for bucket_number in range(bucket_total):
        bucket_sums.append(
            jnp.sum(jnp.where((bucket_grid == bucket_number)[None], bias_grad, 0.0), axis=(1, 2))
        )
    table_local_grad = jnp.stack(bucket_sums)
    table_grad = lax.dynamic_update_slice(
        jnp.zeros((bucket_total, head_total), jnp.float32),
        table_local_grad,
        (jnp.int32(0), mp_index * head_local),
    )
    gains_grad, table_grad = lax.psum(
        (jnp.stack([gain_one_grad, gain_two_grad]), table_grad), ("dp", "mp")
    )
    qkv_sum, attn_out_sum, up_sum, down_sum = (
        lax.psum_scatter(qkv_grad, "dp", scatter_dimension=1, tiled=True),
        lax.psum_scatter(attn_out_grad, "dp", scatter_dimension=1, tiled=True),
        lax.psum_scatter(up_grad, "dp", scatter_dimension=0, tiled=True),
        lax.psum_scatter(down_grad, "dp", scatter_dimension=1, tiled=True),
    )
    qkv_new, qkv_first, qkv_second = adamw(w_qkv, qkv_sum, m_qkv, v_qkv, MATRIX_RATE, WEIGHT_DECAY)
    attn_out_new, attn_out_first, attn_out_second = adamw(
        w_attn_out, attn_out_sum, m_attn_out, v_attn_out, MATRIX_RATE, WEIGHT_DECAY
    )
    up_new, up_first, up_second = adamw(w_up, up_sum, m_up, v_up, MATRIX_RATE, WEIGHT_DECAY)
    down_new, down_first, down_second = adamw(
        w_down, down_sum, m_down, v_down, MATRIX_RATE, WEIGHT_DECAY
    )
    gains_new, gains_first, gains_second = adamw(
        gains, gains_grad, m_gains, v_gains, SMALL_RATE, 0.0
    )
    rel_new, rel_first, rel_second = adamw(rel_table, table_grad, m_rel, v_rel, SMALL_RATE, 0.0)
    return (
        output,
        grad_input,
        qkv_new,
        qkv_first,
        qkv_second,
        qkv_new.astype(jnp.bfloat16),
        attn_out_new,
        attn_out_first,
        attn_out_second,
        attn_out_new.astype(jnp.bfloat16),
        up_new,
        up_first,
        up_second,
        up_new.astype(jnp.bfloat16),
        down_new,
        down_first,
        down_second,
        down_new.astype(jnp.bfloat16),
        gains_new,
        gains_first,
        gains_second,
        rel_new,
        rel_first,
        rel_second,
    )


def solution(mesh):
    placed = (
        P("dp", "mp", None),
        P("dp", "mp", None),
        P("dp", None),
        P("dp"),
        P("dp", None),
        P("dp", None, "mp"),
        P("dp", None, "mp"),
        P(None, "dp", "mp"),
        P(None, "dp", "mp"),
        P(None, "dp", "mp"),
        P("mp", "dp"),
        P("mp", "dp"),
        P("mp", "dp"),
        P("dp", "mp"),
        P("dp", "mp"),
        P("dp", "mp"),
        P("mp", "dp"),
        P("mp", "dp"),
        P("mp", "dp"),
        P(),
        P(),
        P(),
        P(),
        P(),
        P(),
    )
    return jax.shard_map(
        on_device,
        mesh=mesh,
        in_specs=placed,
        out_specs=(
            P("dp", "mp", None),
            P("dp", "mp", None),
            P(None, "dp", "mp"),
            P(None, "dp", "mp"),
            P(None, "dp", "mp"),
            P(None, "dp", "mp"),
            P("mp", "dp"),
            P("mp", "dp"),
            P("mp", "dp"),
            P("mp", "dp"),
            P("dp", "mp"),
            P("dp", "mp"),
            P("dp", "mp"),
            P("dp", "mp"),
            P("mp", "dp"),
            P("mp", "dp"),
            P("mp", "dp"),
            P("mp", "dp"),
            P(),
            P(),
            P(),
            P(),
            P(),
            P(),
        ),
        check_vma=False,
    )
```

profile of v0, /device:TPU:25, one launch (start us, length us, event | category | flops | bytes accessed | tf_op | source)
XLA Modules:
  0.0 1095.2 jit_solution(6395958381325415294)
XLA Ops:
  59.9 6.6 broadcast_compare_fusion.16
  110.7 54.1 %select_add_fusion.1 = f32[3,1024,1024]{2,1,0:T(8,128)} fusion(f32[3]{0:T(128)S(1)} %get-tuple-element.430, f32[3]{0:T(128)S(1)} %get-tuple-element.431, f32[3]{0:T(128)S(1)} %get-tuple-element.432, f32[3]{0:T(128)S(1)} %get-tuple-element.433, f32[3]{0:T(128)S(1)} %get-tuple-element.434, f32[3]{0:T(128)S(1)} %get-tuple-element.435, ...), kind=kLoop, calls=%fused_computation.211 | loop fusion | flops 198180864 | bytes 46137728 | tf_op jit(solution)/shard_map/add | solution.py:118
  166.5 10.1 all_gather.26
  176.7 11.8 %all_gather.25 = bf16[3,768,192]{2,1,0:T(8,128)(2,1)S(1)} all-gather(bf16[3,96,192]{2,1,0:T(8,128)(2,1)S(1)} %convert_element_type.1706), channel_id=1, replica_groups=mesh['dp'=8,'mp'=4] {'dp'}, dimensions={1}, use_global_device_ids=true | all-gather | bytes 995328 | tf_op jit(solution)/shard_map/all_gather | solution.py:98
  195.5 53.3 %while.29 = (s32[]{:T(128)}, bf16[2,3,1024,64]{2,3,1,0:T(8,128)(2,1)S(1)}, f32[2,3,1024]{2,1,0:T(4,128)}, s32[2]{0:T(128)}, s32[2,16]{1,0:T(2,128)S(1)}, /*index...) while((s32[]{:T(128)}, ...), condition=%wide.region_10.11_spmd, body=%wide.region_1.10_spmd.sunk | while | flops 861836288 | bytes 99863008 | solution.py:175
  254.1 108.2 %reduce-scatter.13.cloned.1.call-done = f32[2,256,768]{2,1,0:T(8,128)} async-done(((f32[2,1024,768]{2,1,0:T(8,128)}), f32[2,256,768]{2,1,0:T(8,128)}) %reduce-scatter.13.cloned.1.call-update) | async-done | bytes 1572880 | tf_op jit(solution)/shard_map/reduce_scatter | solution.py:182
  366.0 61.4 %all-gather.9.cloned.1.call-done = bf16[2,1024,768]{2,1,0:T(8,128)(2,1)} async-done(((bf16[2,256,768]{2,1,0:T(8,128)(2,1)}), bf16[2,1024,768]{2,1,0:T(8,128)(2,1)}) %all-gather.9.cloned.1.call-update) | async-done | bytes 3145744 | tf_op jit(solution)/shard_map/all_gather | solution.py:187
  427.5 6.7 fusion.171
  436.7 15.3 %multiply_convert_fusion.6 = (bf16[2,1024,768]{2,1,0:T(8,128)(2,1)}, f32[2,1024,768]{2,1,0:T(8,128)}) fusion(f32[2,1024,768]{2,1,0:T(8,128)S(1)} %get-tuple-element.589, u8[1024,768]{1,0:T(8,128)(4,1)S(1)} %get-tuple-element.422, u8[1024,768]{1,0:T(8,128)(4,1)S(1)} %get-tuple-element.421), kind=kLoop, calls=%fused_computation.222 | loop fusion | flops 110100480 | bytes 17301504 | tf_op jit(solution)/shard_map/convert_element_type | solution.py:191
  452.0 38.9 %all-gather.15.cloned.1.call-done = bf16[2,1024,768]{2,1,0:T(8,128)(2,1)} async-done(((bf16[2,256,768]{2,1,0:T(8,128)(2,1)}), bf16[2,1024,768]{2,1,0:T(8,128)(2,1)}) %all-gather.15.cloned.1.call-update) | async-done | bytes 3145744 | tf_op jit(solution)/shard_map/all_gather | solution.py:198
  490.9 6.9 convolution_bitcast_fusion.1
  497.9 43.3 %reduce-scatter.23.cloned.1.call-done = f32[768,96]{0,1:T(8,128)} async-done(((f32[768,768]{0,1:T(8,128)}), f32[768,96]{0,1:T(8,128)}) %reduce-scatter.23.cloned.1.call-update) | async-done | bytes 294928 | tf_op jit(solution)/shard_map/reduce_scatter | solution.py:325
  543.8 24.6 %all-gather.13.cloned.1.call-done = bf16[768,768]{0,1:T(8,128)(2,1)} async-done(((bf16[768,96]{0,1:T(8,128)(2,1)}), bf16[768,768]{0,1:T(8,128)(2,1)}) %all-gather.13.cloned.1.call-update) | async-done | bytes 1179664 | tf_op jit(solution)/shard_map/all_gather | solution.py:101
  568.4 10.1 add_convert_fusion
  584.8 109.7 %reduce-scatter.17.cloned.1.call-done = f32[2,256,768]{2,1,0:T(8,128)} async-done(((f32[2,1024,768]{2,1,0:T(8,128)}), f32[2,256,768]{2,1,0:T(8,128)}) %reduce-scatter.17.cloned.1.call-update) | async-done | bytes 1572880 | tf_op jit(solution)/shard_map/reduce_scatter | solution.py:206
  699.2 7.0 convolution_bitcast_fusion.2
  706.2 55.2 %all-gather.17.cloned.1.call-done = bf16[2,1024,768]{2,1,0:T(8,128)(2,1)} async-done(((bf16[2,256,768]{2,1,0:T(8,128)(2,1)}), bf16[2,1024,768]{2,1,0:T(8,128)(2,1)}) %all-gather.17.cloned.1.call-update) | async-done | bytes 3145744 | tf_op jit(solution)/shard_map/all_gather | solution.py:210
  772.3 133.1 %while.30 = (s32[]{:T(128)}, f32[3,1024,1024]{2,1,0:T(8,128)}, bf16[2,3,1024,64]{2,3,1,0:T(8,128)(2,1)}, bf16[2,3,1024,64]{2,3,1,0:T(8,128)(2,1)}, bf16[2,3,1024...) while((s32[]{:T(128)}, f32[3,1024,1024]{2,1,0:T(8,128)}, ...), condition=%wide.region_21.22_spmd.clone, body=%wide.region_16.21_spmd.clone.sunk | while | flops 2105575424 | bytes 350465216 | solution.py:278
  814.2 7.0 multiply_convert_fusion.14
  877.7 7.0 multiply_convert_fusion.14
  893.5 11.7 %select_add_fusion.3 = f32[3,1024,1024]{2,1,0:T(8,128)} fusion(f32[3,1024,1024]{2,1,0:T(8,128)} %get-tuple-element.922, bf16[3,512,1024]{2,1,0:T(8,128)(2,1)S(1)} %copy-done.4, bf16[3,512,1024]{2,1,0:T(8,128)(2,1)S(1)} %multiply_convert_fusion.15, pred[]{:T(512)S(6)} %compare.3), kind=kLoop, calls=%fused_computation.71.clone.1 | loop fusion | flops 18874368 | bytes 31457280 | tf_op jit(solution)/shard_map/while/body/eval_jaxpr/add | solution.py:270
  936.7 37.9 %select_reduce_fusion = (f32[3]{0:T(128)S(1)}, f32[3]{0:T(128)S(1)}, f32[3]{0:T(128)S(1)}, f32[3]{0:T(128)S(1)}, f32[3]{0:T(128)S(1)}, /*index=5*/f32[3]{0:T(128...) fusion(f32[3,1024,1024]{2,1,0:T(8,128)} %get-tuple-element.177,, ...), kind=kLoop, calls=%fused_computation.179 | loop fusion | flops 113246168 | bytes 31457496 | tf_op jit(solution)/shard_map/reduce_sum | solution.py:310
  974.9 29.9 %select_reduce_fusion.1 = (f32[3]{0:T(128)S(1)}, f32[3]{0:T(128)S(1)}, f32[3]{0:T(128)S(1)}, f32[3]{0:T(128)S(1)}, f32[3]{0:T(128)S(1)}, /*index=5*/f32[3]{0:T(1...) fusion(f32[3,1024,1024]{2,1,0:T(8,128)} %get-tuple-element.177,, ...), kind=kLoop, calls=%fused_computation.180 | loop fusion | flops 88080344 | bytes 27263144 | tf_op jit(solution)/shard_map/reduce_sum | solution.py:310
  1034.7 44.7 %all-reduce = (f32[2,768]{1,0:T(2,128)S(1)}, f32[32,12]{0,1:T(8,128)S(1)}) all-reduce(f32[2,768]{1,0:T(2,128)S(1)} %pad_maximum_fusion.1, f32[32,12]{0,1:T(8,128)S(1)} %copy-done.68), channel_id=1, replica_groups=mesh['dp'=8,'mp'=4] {'dp','mp'}, use_global_device_ids=true, to_apply=%region_30.31 | all-reduce | flops 1920 | bytes 15360 | tf_op jit(solution)/shard_map/psum | solution.py:318
  (509 shorter events, 368.5 us)
Async XLA Ops:
  8.0 181.6 %all-gather.7.cloned.1.call-start = ((), (), s32[]{:S(2)}) async-start(), calls=%async_computation.8 | async-start | bytes 3932160 | tf_op jit(solution)/shard_map/all_gather | solution.py:127
  13.7 348.6 %reduce-scatter.13.cloned.1.call-start = ((), (), s32[]{:S(2)}) async-start(), calls=%async_computation.9 | async-start | bytes 7864320 | tf_op jit(solution)/shard_map/reduce_scatter | solution.py:182
  20.7 89.9 %copy-start.21 = (pred[1024,1024]{1,0:T(8,128)(4,1)}, pred[1024,1024]{1,0:T(8,128)(4,1)S(1)}, u32[]{:S(2)}) copy-start(pred[1024,1024]{1,0:T(8,128)(4,1)S(1)} %get-tuple-element.620) | copy-start | bytes 3145732
  20.7 89.9 %copy-start.23 = (pred[1024,1024]{1,0:T(8,128)(4,1)}, pred[1024,1024]{1,0:T(8,128)(4,1)S(1)}, u32[]{:S(2)}) copy-start(pred[1024,1024]{1,0:T(8,128)(4,1)S(1)} %get-tuple-element.621) | copy-start | bytes 3145732
  32.2 78.4 %copy-start.25 = (pred[1024,1024]{1,0:T(8,128)(4,1)}, pred[1024,1024]{1,0:T(8,128)(4,1)S(1)}, u32[]{:S(2)}) copy-start(pred[1024,1024]{1,0:T(8,128)(4,1)S(1)} %get-tuple-element.616) | copy-start | bytes 3145732
  32.2 78.4 %copy-start.27 = (pred[1024,1024]{1,0:T(8,128)(4,1)}, pred[1024,1024]{1,0:T(8,128)(4,1)S(1)}, u32[]{:S(2)}) copy-start(pred[1024,1024]{1,0:T(8,128)(4,1)S(1)} %get-tuple-element.617) | copy-start | bytes 3145732
  252.4 109.9 %copy-start.16 = (bf16[2,256,768]{2,1,0:T(8,128)(2,1)S(1)}, bf16[2,256,768]{2,1,0:T(8,128)(2,1)}, u32[]{:S(2)}) copy-start(bf16[2,256,768]{2,1,0:T(8,128)(2,1)} %param.29) | copy-start | bytes 2359300
  252.4 111.6 %copy-start.57 = (f32[768]{0:T(1024)S(1)}, f32[768]{0:T(1024)}, u32[]{:S(2)}) copy-start(f32[768]{0:T(1024)} %get-tuple-element.427) | copy-start | bytes 9220
  252.4 113.6 %all-gather.11.cloned.1.call-start = ((), (), s32[]{:S(2)}) async-start(), calls=%async_computation.11 | async-start | bytes 1327104 | tf_op jit(solution)/shard_map/all_gather | solution.py:100
  254.1 173.4 %all-gather.9.cloned.1.call-start = ((), (), s32[]{:S(2)}) async-start(), calls=%async_computation.10 | async-start | bytes 3932160 | tf_op jit(solution)/shard_map/all_gather | solution.py:187
  364.0 333.1 %copy-start.14 = (f32[2,256,768]{2,1,0:T(8,128)}, f32[2,256,768]{2,1,0:T(8,128)S(1)}, u32[]{:S(2)}) copy-start(f32[2,256,768]{2,1,0:T(8,128)S(1)} %get-tuple-element.552) | copy-start | bytes 4718596
  364.0 333.1 %copy-start.63 = (f32[2,256]{1,0:T(2,128)}, f32[2,256]{1,0:T(2,128)S(1)}, u32[]{:S(2)}) copy-start(f32[2,256]{1,0:T(2,128)S(1)} %add_rsqrt_fusion) | copy-start | bytes 6148
  365.4 125.6 %all-gather.15.cloned.1.call-start = ((), (), s32[]{:S(2)}) async-start(), calls=%async_computation.14 | async-start | bytes 3932160 | tf_op jit(solution)/shard_map/all_gather | solution.py:198
  365.9 175.3 %reduce-scatter.23.cloned.1.call-start = ((), (), s32[]{:S(2)}) async-start(), calls=%async_computation.19 | async-start | bytes 2654208 | tf_op jit(solution)/shard_map/reduce_scatter | solution.py:325
  497.9 70.5 %all-gather.13.cloned.1.call-start = ((), (), s32[]{:S(2)}) async-start(), calls=%async_computation.12 | async-start | bytes 1327104 | tf_op jit(solution)/shard_map/all_gather | solution.py:101
  543.5 151.0 %reduce-scatter.17.cloned.1.call-start = ((), (), s32[]{:S(2)}) async-start(), calls=%async_computation.15 | async-start | bytes 7864320 | tf_op jit(solution)/shard_map/reduce_scatter | solution.py:206
  584.7 113.0 %copy-start.37 = (bf16[2,256,768]{2,1,0:T(8,128)(2,1)S(1)}, bf16[2,256,768]{2,1,0:T(8,128)(2,1)}, u32[]{:S(2)}) copy-start(bf16[2,256,768]{2,1,0:T(8,128)(2,1)} %param.30) | copy-start | bytes 2359300
  584.8 176.7 %all-gather.17.cloned.1.call-start = ((), (), s32[]{:S(2)}) async-start(), calls=%async_computation.16 | async-start | bytes 3932160 | tf_op jit(solution)/shard_map/all_gather | solution.py:210
  699.1 234.7 %reduce-scatter.21.cloned.1.call-start = ((), (), s32[]{:S(2)}) async-start(), calls=%async_computation.18 | async-start | bytes 2654208 | tf_op jit(solution)/shard_map/reduce_scatter | solution.py:324
  706.2 312.9 %reduce-scatter.27.cloned.1.call-start = ((), (), s32[]{:S(2)}) async-start(), calls=%async_computation.21 | async-start | bytes 884736
  765.3 256.1 %reduce-scatter.25.cloned.1.call-start = ((), (), s32[]{:S(2)}) async-start(), calls=%async_computation.20 | async-start | bytes 2211840
  917.2 115.0 %reduce-scatter.19.cloned.1.call-start = ((), (), s32[]{:S(2)}) async-start(), calls=%async_computation.17 | async-start | bytes 3932160 | tf_op jit(solution)/shard_map/reduce_scatter | solution.py:302
  923.6 160.0 %reduce-scatter.15.cloned.1.call-start = ((), (), s32[]{:S(2)}) async-start(), calls=%async_computation.13 | async-start | bytes 3932160 | tf_op jit(solution)/shard_map/reduce_scatter | solution.py:193
  1010.1 73.5 %copy-start.64 = (f32[2,256]{1,0:T(2,128)S(1)}, f32[2,256]{1,0:T(2,128)}, u32[]{:S(2)}) copy-start(f32[2,256]{1,0:T(2,128)} %copy-done.63) | copy-start | bytes 6148
  (105 other events, 2233.3 us)
Sparse Core Ops, SparseCore 0:
  13.8 62.0 all-gather.6
  252.6 109.7 reduce-scatter.12
  699.2 62.1 all-gather.16
Sparse Core Ops, SparseCore 1:
  255.4 23.8 all-gather.10
  365.4 62.0 all-gather.8
  428.9 62.0 all-gather.14
  498.0 43.3 reduce-scatter.22
  543.9 24.4 all-gather.12
  584.8 109.6 reduce-scatter.16
  706.3 43.3 reduce-scatter.20
  765.4 35.5 reduce-scatter.26
  917.3 41.0 reduce-scatter.24
  960.8 59.2 reduce-scatter.18
  1022.3 61.2 reduce-scatter.14
where the time goes:
time: 1110 us; the launch traced here: 1100 us
  waiting for transfers between devices  445 us (40%)
  other arithmetic  323 us (29%)
  matrix products  166 us (15%)
  local copies, waits for them, and re-layouts  75.1 us (7%)
  blocking collectives  66.7 us (6%)
  between operations  16.6 us (1%)
    reduce_scatter x1, waiting for transfers between devices, on_device(): lax.psum_scatter(grad_normed_part, 'mp', scatter_dimension=1, tiled=True)  110 us
    reduce_scatter x1, waiting for transfers between devices, on_device(): lax.psum_scatter(attn_term, 'mp', scatter_dimension=1, tiled=True)  108 us
    eq x16, other arithmetic, on_device(): bucket_grid == bucket_number  95.1 us
    reduce_sum x2, other arithmetic, on_device(): jnp.sum(jnp.where((bucket_grid == bucket_number)[None], bias_grad, 0.0),...  67.8 us
    all_gather x1, waiting for transfers between devices, on_device(): ffn_source = lax.all_gather(normed_two, 'mp', axis=1, tiled=True)  61.4 us
    all_gather x1, waiting for transfers between devices, on_device(): grad_attn_full = lax.all_gather(grad_mid_low, 'mp', axis=1, tiled=True)  55.2 us
    add x1, other arithmetic, on_device(): rel_bias + jnp.where((bucket_grid == bucket_number)[None], table_local[bu...  54.1 us
    psum x1, blocking collectives, on_device(): lax.psum((jnp.stack([gain_one_grad, gain_two_grad]), table_grad), ('dp',...  44.7 us
  transfers between devices with their start and end apart: 14, of which 8 were waited for; matrix products, arithmetic and copies ran while one was open for 41% of the time, Pallas kernels for 0%

commit v1 on v0

--- a/solution.py
+++ b/solution.py
@@ -1,6 +1,12 @@
+import functools
+
 import jax
 import jax.numpy as jnp
+import numpy as np
 from jax import lax
+from jax.experimental import pallas as pl
+from jax.experimental.pallas import tpu as pltpu
+from jax.sharding import Mesh
 from jax.sharding import PartitionSpec as P
 
 HEAD_DIM = 64
@@ -364,27 +370,920 @@
     )
 
 
+BF = jnp.bfloat16
+F32 = jnp.float32
+MESH_ID = pl.DeviceIdType.MESH
+BIG = 1e30
+KEY_PAD = 128
+WIDE = 256
+SQRT_HALF = 0.5**0.5
+INV_SQRT_2PI = 0.3989422804014327
+LINK_SEMS = 160
+VMEM_LIMIT = 63 * 2**20
+
+
+def dot(a, b):
+    return lax.dot_general(a, b, (((1,), (0,)), ((), ())), preferred_element_type=F32)
+
+
+def dot_t(a, b):
+    return lax.dot_general(a, b, (((1,), (1,)), ((), ())), preferred_element_type=F32)
+
+
+def split3(v):
+    hi = v.astype(BF)
+    rest = v - hi.astype(F32)
+    mid = rest.astype(BF)
+    low = (rest - mid.astype(F32)).astype(BF)
+    return hi, mid, low
+
+
+class Links:
+    def __init__(self, send_sems, recv_sems):
+        self.send_sems, self.recv_sems = send_sems, recv_sems
+        self.count = 0
+        self.sent = []
+
+    def send(self, src, dst, device):
+        k = self.count
+        self.count += 1
+        copy = pltpu.make_async_remote_copy(
+            src, dst, self.send_sems.at[k], self.recv_sems.at[k], device_id=device, device_id_type=MESH_ID
+        )
+        copy.start()
+        self.sent.append(copy)
+        return k
+
+    def send_or_keep(self, src, dst, device, is_self, send_at, recv_at):
+        copy = pltpu.make_async_remote_copy(
+            src, dst, self.send_sems.at[send_at], self.recv_sems.at[recv_at], device_id=device, device_id_type=MESH_ID
+        )
+
+        @pl.when(is_self)
+        def _():
+            pltpu.make_async_copy(src, dst, self.recv_sems.at[recv_at]).start()
+
+        @pl.when(jnp.logical_not(is_self))
+        def _():
+            copy.start()
+
+        self.sent.append((copy, is_self))
+
+    def send_unless(self, src, dst, device, is_self, send_at, recv_at):
+        copy = pltpu.make_async_remote_copy(
+            src, dst, self.send_sems.at[send_at], self.recv_sems.at[recv_at], device_id=device, device_id_type=MESH_ID
+        )
+
+        @pl.when(jnp.logical_not(is_self))
+        def _():
+            copy.start()
+
+        self.sent.append((copy, is_self))
+
+    def arrived(self, dst, k):
+        pltpu.make_async_copy(dst, dst, self.recv_sems.at[k]).wait()
+
+    def drain(self):
+        for item in self.sent:
+            if isinstance(item, tuple):
+                copy, is_self = item
+
+                @pl.when(jnp.logical_not(is_self))
+                def _(copy=copy):
+                    copy.wait_send()
+
+            else:
+                item.wait_send()
+        self.sent = []
+
+
+class Place:
+    def __init__(self):
+        self.y, self.x = lax.axis_index("y"), lax.axis_index("x")
+        self.c, self.z = lax.axis_index("c"), lax.axis_index("z")
+        self.to_x, self.to_y = {"x": 1 - self.x}, {"y": 1 - self.y}
+        self.to_c = {"c": 1 - self.c}
+
+    def to_z(self, k):
+        return {"z": lax.rem(self.z + k, 4)}
+
+    def from_z(self, k):
+        return lax.rem(self.z + 4 - k, 4)
+
+    def greet(self):
+        barrier = pltpu.get_barrier_semaphore()
+        peers = [self.to_x, self.to_y, self.to_c]
+        for k in (1, 2, 3):
+            peers.append(self.to_z(k))
+            peers.append({"z": lax.rem(self.z + k, 4), "c": 1 - self.c})
+        for peer in peers:
+            pl.semaphore_signal(barrier, inc=1, device_id=peer, device_id_type=MESH_ID)
+        pl.semaphore_wait(barrier, len(peers))
+
+
+class Gather:
+    def __init__(self, place, links, shard, whole, local_sem):
+        self.p, self.links, self.shard, self.whole, self.local_sem = place, links, shard, whole, local_sem
+
+    @staticmethod
+    def rows(y, x, c):
+        return y * 4 + x * 2 + c
+
+    def start_z(self):
+        p, links = self.p, self.links
+        own = self.whole.at[p.z, self.rows(p.y, p.x, p.c)]
+        self.own_copy = pltpu.make_async_copy(self.shard, own, self.local_sem)
+        self.own_copy.start()
+        self.k_z = {k: links.send(self.shard, own, p.to_z(k)) for k in (2, 1, 3)}
+
+    def start_xy(self):
+        p, links = self.p, self.links
+        own = self.whole.at[p.z, self.rows(p.y, p.x, p.c)]
+        self.k_x = {0: links.send(self.shard, own, p.to_x)}
+        self.k_y = {0: links.send(self.shard, own, p.to_y)}
+
+    def column(self):
+        p, links = self.p, self.links
+        for k in (1, 3, 2):
+            block = self.whole.at[p.from_z(k), self.rows(p.y, p.x, p.c)]
+            links.arrived(block, self.k_z[k])
+            self.k_x[k] = links.send(block, block, p.to_x)
+            self.k_y[k] = links.send(block, block, p.to_y)
+        self.own_copy.wait()
+        block = self.whole.at[:, self.rows(p.y, p.x, p.c)]
+        self.k_c = [links.send(block, block, p.to_c)]
+
+    def plane(self):
+        p, links = self.p, self.links
+        self.k_d = {}
+        for k in (0, 1):
+            block = self.whole.at[p.from_z(k), self.rows(p.y, 1 - p.x, p.c)]
+            links.arrived(block, self.k_x[k])
+            self.k_d[k] = links.send(block, block, p.to_y)
+        for k in (3, 2):
+            block = self.whole.at[p.from_z(k), self.rows(1 - p.y, p.x, p.c)]
+            links.arrived(block, self.k_y[k])
+            self.k_d[k] = links.send(block, block, p.to_x)
+        for k in (3, 2):
+            links.arrived(self.whole.at[p.from_z(k), self.rows(p.y, 1 - p.x, p.c)], self.k_x[k])
+        for k in (0, 1):
+            links.arrived(self.whole.at[p.from_z(k), self.rows(1 - p.y, p.x, p.c)], self.k_y[k])
+        for y, x in ((p.y, 1 - p.x), (1 - p.y, p.x)):
+            block = self.whole.at[:, self.rows(y, x, p.c)]
+            self.k_c.append(links.send(block, block, p.to_c))
+
+    def corner(self):
+        p, links = self.p, self.links
+        for k in (0, 1, 3, 2):
+            links.arrived(self.whole.at[p.from_z(k), self.rows(1 - p.y, 1 - p.x, p.c)], self.k_d[k])
+        block = self.whole.at[:, self.rows(1 - p.y, 1 - p.x, p.c)]
+        self.k_c.append(links.send(block, block, p.to_c))
+
+    def finish(self):
+        p = self.p
+        spots = ((p.y, p.x), (p.y, 1 - p.x), (1 - p.y, p.x), (1 - p.y, 1 - p.x))
+        for (y, x), k in zip(spots, self.k_c):
+            self.links.arrived(self.whole.at[:, self.rows(y, x, 1 - p.c)], k)
+
+
+class Reduce:
+    def __init__(self, place, links, grads, land):
+        self.p, self.links, self.g, self.land = place, links, grads, land
+        self.k_c, self.k_first, self.k_second = {}, {}, {}
+        self.at_z = links.count
+        links.count += 4
+
+    def start(self, q):
+        p = self.p
+        spot = self.land.at[q // 2, pl.ds(q % 2 * 4, 4)]
+        self.k_c[q] = self.links.send(self.g.at[q, :, 1 - p.c], spot, p.to_c)
+
+    def add(self, q, n, row, col):
+        at = (q, n, self.p.c)
+        self.g[at] = (self.g[at].astype(F32) + self.land[row, col].astype(F32)).astype(BF)
+
+    def core(self, q):
+        p, links = self.p, self.links
+        links.arrived(self.land.at[q // 2, pl.ds(q % 2 * 4, 4)], self.k_c[q])
+        for n in range(4):
+            self.add(q, n, q // 2, q % 2 * 4 + n)
+        self.k_first[q] = []
+        for i in (0, 1):
+            n, peer = (2 * i + 1 - p.x, p.to_x) if q < 2 else (2 * (1 - p.y) + i, p.to_y)
+            self.k_first[q].append(links.send(self.g.at[q, n, p.c], self.land.at[2, 2 * q + i], peer))
+
+    def plane(self, q):
+        p, links = self.p, self.links
+        for i in (0, 1):
+            links.arrived(self.land.at[2, 2 * q + i], self.k_first[q][i])
+            self.add(q, 2 * i + p.x if q < 2 else 2 * p.y + i, 2, 2 * q + i)
+        n, peer = (2 * (1 - p.y) + p.x, p.to_y) if q < 2 else (2 * p.y + 1 - p.x, p.to_x)
+        self.k_second[q] = links.send(self.g.at[q, n, p.c], self.land.at[3, q], peer)
+
+    def column(self, q):
+        p, links = self.p, self.links
+        here = 2 * p.y + p.x
+        links.arrived(self.land.at[3, q], self.k_second[q])
+        self.add(q, here, 3, q)
+        links.send_unless(
+            self.g.at[q, here, p.c], self.land.at[3, 4 + p.z], {"z": q}, p.z == q, self.at_z + q, self.at_z + p.z
+        )
+
+    def finish(self, out):
+        p = self.p
+        total = self.g[p.z, 2 * p.y + p.x, p.c].astype(F32)
+        for k in (1, 2, 3):
+            source = p.from_z(k)
+            self.links.arrived(self.land.at[3, 4 + source], self.at_z + source)
+            total = total + self.land[3, 4 + source].astype(F32)
+        out[...] = total
+
+
+def band_tiles(group, chunk):
+    tiles = []
+    for i in range(2):
+        for j in range(2):
+            block = 2 * group + j
+            if chunk < 2:
+                apart = 2 * chunk + i - block
+                if abs(apart) <= 1:
+                    tiles.append((i, j, apart + 1, None))
+            else:
+                other = 2 * (chunk - 2) + i
+                if block == 3 and other == 0:
+                    tiles.append((i, j, 2, 0))
+                if block == 0 and other == 3:
+                    tiles.append((i, j, 0, 1))
+    return tiles
+
+
+def add_band(s, band, group, chunk, core):
+    tiles = band_tiles(group, chunk)
+    if not tiles:
+        return s
+    rows = []
+    for i in range(2):
+        cols = []
+        for j in range(2):
+            part = s[i * 128 : (i + 1) * 128, j * 128 : (j + 1) * 128]
+            for a, b, third, need in tiles:
+                if (a, b) == (i, j):
+                    near = band[third * 128 : (third + 1) * 128, :]
+                    if need is not None:
+                        near = near * jnp.where(core == need, 1.0, 0.0)
+                    part = part + near
+            cols.append(part)
+        rows.append(jnp.concatenate(cols, axis=1))
+    return jnp.concatenate(rows, axis=0)
+
+
+def far_masks(core, span):
+    key = lax.broadcasted_iota(jnp.int32, (8, span), 0)
+    block = lax.broadcasted_iota(jnp.int32, (8, span), 1) // 128
+    other = key - 4
+    left = ((key < 4) & (key <= block - 2)) | ((key >= 4) & (core == 1) & ~((block == 0) & (other == 3)))
+    right = ((key < 4) & (key >= block + 2)) | ((key >= 4) & (core == 0) & ~((block == 3) & (other == 0)))
+    return left, right
+
+
+def rows_of(parts, span):
+    row = lax.broadcasted_iota(jnp.int32, (8, span), 0)
+    out = jnp.zeros((8, span), F32)
+    for n, part in enumerate(parts):
+        out = jnp.where(row == n, part.astype(F32), out)
+    return out.astype(BF)
+
+
+def far_rows(left, right, far_left, far_right):
+    hi, mid, low = split3(jnp.where(left, far_left, jnp.where(right, far_right, 0.0)))
+    return jnp.concatenate([hi.astype(F32), mid.astype(F32), low.astype(F32)], axis=0).astype(BF)
+
+
+def fwd_head(R, h, core, far_left, far_right):
+    span, keys = R.QT.shape[2], R.KVT.shape[2]
+    toks = keys - KEY_PAD
+    R.ka[0:64, :] = R.KVT[h, 0:64, :]
+    R.Ka[...] = R.ka[...].T
+    R.va[0:64, :] = R.KVT[h, 64:128, :]
+    R.qa[0:64, :] = R.QT[h]
+    left, right = far_masks(core, span)
+    R.qa[80:104, :] = far_rows(left, right, far_left, far_right)
+    R.band[...] = band_of(R.wave[pl.ds(h, 1), :])
+    band = R.band
+    chunks = [(n, slice(n * WIDE, (n + 1) * WIDE)) for n in range(toks // WIDE)]
+    last = slice(toks, toks + 32)
+    for group in range(span // WIDE):
+        cols = slice(group * WIDE, (group + 1) * WIDE)
+        query = R.qa[:, cols]
+        peak = None
+        for n, rows in chunks:
+            s = add_band(dot(R.Ka[rows, :], query), band, group, n, core)
+            R.S[rows, :] = s
+            top = jnp.max(s, axis=0, keepdims=True)
+            peak = top if peak is None else jnp.maximum(peak, top)
+        s = dot(R.Ka[last, :], query)
+        R.S[last, :] = s
+        peak = jnp.maximum(peak, jnp.max(s, axis=0, keepdims=True))
+        for _, rows in chunks:
+            R.P[rows, :] = jnp.exp(R.S[rows, :] - peak).astype(BF)
+        R.P[last, :] = jnp.exp(R.S[last, :] - peak).astype(BF)
+        o = dot(R.va[0:72, :], R.P[...])
+        total = o[64:65, :]
+        R.ctxT[h, :, cols] = (o[0:64, :] * (1.0 / total)).astype(BF)
+        R.lse[pl.ds(h, 1), cols] = peak + jnp.log(total)
+
+
+def bwd_head(R, h, j, core, far_left, far_right):
+    span, keys = R.QT.shape[2], R.KVT.shape[2]
+    toks = keys - KEY_PAD
+    R.ka[0:64, :] = R.KVT[h, 0:64, :]
+    R.Ka[...] = R.ka[...].T
+    R.va[0:64, :] = R.KVT[h, 64:128, :]
+    R.Va[...] = R.va[...].T
+    R.qa[0:64, :] = R.QT[h]
+    left, right = far_masks(core, span)
+    R.qa[80:104, :] = far_rows(left, right, far_left, far_right)
+    R.qa[72:80, :] = rows_of(split3(-R.lse[pl.ds(h, 1), :]), span)
+    grad = R.dOT[h]
+    R.da[0:64, :] = grad
+    row_dot = jnp.sum(grad.astype(F32) * R.ctxT[h].astype(F32), axis=0, keepdims=True)
+    R.da[64:72, :] = rows_of(split3(-row_dot), span)
+    R.band[...] = band_of(R.wave[pl.ds(h, 1), :])
+    band = R.band
+    groups = span // WIDE
+    query_sum = [None] * groups
+    near = [None, None, None]
+    for n in range(toks // WIDE + 1):
+        is_mem = n * WIDE == toks
+        rows = slice(toks, toks + 32) if is_mem else slice(n * WIDE, (n + 1) * WIDE)
+        key_sum = value_sum = None
+        for group in range(groups):
+            cols = slice(group * WIDE, (group + 1) * WIDE)
+            s = dot(R.Ka[rows, :], R.qa[:, cols])
+            if not is_mem:
+                s = add_band(s, band, group, n, core)
+            p = jnp.exp(s)
+            ds = p * dot(R.Va[rows, :], R.da[:, cols])
+            ds_low = ds.astype(BF)
+            if is_mem:
+                filled = jnp.concatenate([ds_low, jnp.zeros((KEY_PAD - 32, WIDE), BF)], axis=0)
+                part = dot(R.ka[0:96, toks:keys], filled)
+            else:
+                v = dot_t(p.astype(BF), R.da[0:64, cols])
+                k = dot_t(ds_low, R.qa[0:64, cols])
+                value_sum = v if value_sum is None else value_sum + v
+                key_sum = k if key_sum is None else key_sum + k
+                for a, b, third, need in band_tiles(group, n):
+                    t = ds[a * 128 : (a + 1) * 128, b * 128 : (b + 1) * 128]
+                    if need is not None:
+                        t = t * jnp.where(core == need, 1.0, 0.0)
+                    near[third] = t if near[third] is None else near[third] + t
+                part = dot(R.ka[0:96, rows], ds_low)
+            query_sum[group] = part if query_sum[group] is None else query_sum[group] + part
+        if not is_mem:
+            both = jnp.concatenate([key_sum, value_sum], axis=1)
+            if n * WIDE < span:
+                R.kv_own[j, rows, :] = both
+            else:
+                R.kv_out[h, slice(n * WIDE - span, (n + 1) * WIDE - span), :] = both.astype(BF)
+    turned = jnp.concatenate(query_sum, axis=1)
+    R.dq[j] = (turned[0:64, :] * HEAD_DIM**-0.5).T.astype(BF)
+    far = turned[80:88, :]
+    lane = lax.broadcasted_iota(jnp.int32, (1, 128), 1)
+    sum_left = jnp.sum(jnp.where(left, far, 0.0))
+    sum_right = jnp.sum(jnp.where(right, far, 0.0))
+    ends = jnp.where(lane == 0, sum_left, jnp.where(lane == 1, sum_right, 0.0))
+    R.small[pl.ds(8 + h, 1), 0:640] = jnp.concatenate([unband(jnp.concatenate(near, axis=0)), ends], axis=1)
+
+
+class Refs:
+    def __init__(self, **refs):
+        self.__dict__.update(refs)
+
+
+def weights(R, n, z, cols):
+    part = R.W[n, z, :, :, cols]
+    return part.reshape(part.shape[0] * part.shape[1], part.shape[2])
+
+
+class RowMove:
+    def __init__(self, place, links, src, dst):
+        self.links, self.dst = links, dst
+        slot = lax.rem(place.z, 2)
+        at = links.count
+        links.count += 2
+        for i in (0, 1):
+            target_z, target_c = 2 * place.c + i, place.z // 2
+            links.send_or_keep(
+                src.at[i],
+                dst.at[slot],
+                {"c": target_c, "z": target_z},
+                (target_c == place.c) & (target_z == place.z),
+                at + i,
+                at + slot,
+            )
+        self.at = at
+
+    def wait(self, slot):
+        self.links.arrived(self.dst.at[slot], self.at + slot)
+
+
+def norm_parts(values):
+    inverse = lax.rsqrt(jnp.mean(values * values, axis=-1, keepdims=True) + NORM_EPS)
+    return inverse, values * inverse
+
+
+def mask_rows(R, place):
+    span, keys = R.QT.shape[2], R.KVT.shape[2]
+    toks = keys - KEY_PAD
+    mine = jnp.where(place.z // 2 == place.c, R.code[lax.rem(place.z, 2)], R.code_in[...])
+    R.code_in[...] = mine
+    own = R.code_in[:, pl.ds(pl.multiple_of(place.c * span, span), span)]
+    other = R.code_in[:, pl.ds(pl.multiple_of((1 - place.c) * span, span), span)]
+    line = jnp.concatenate([own, other, R.code_in[:, toks:keys]], axis=1)
+    row = lax.broadcasted_iota(jnp.int32, (8, keys), 0)
+    as_doc = (row - 1).astype(F32)
+    kind = jnp.where(row < 5, jnp.where(line == as_doc, 1.0, 0.0), 0.0)
+    kind = jnp.where((row == 5) & (line == 11.0), 1.0, kind)
+    kind = jnp.where((row == 6) & (line >= 10.0), 1.0, kind)
+    R.ka[64:72, :] = kind.astype(BF)
+    R.ka[72:80, :] = jnp.where(row < 3, 1.0, 0.0).astype(BF)
+    block = lax.broadcasted_iota(jnp.int32, (8, keys), 1) // 128
+    hot = jnp.where((block == row) & (block < toks // 128), 1.0, 0.0)
+    R.ka[80:104, :] = jnp.concatenate([hot, hot, hot], axis=0).astype(BF)
+    R.ka[104:128, :] = jnp.zeros((24, keys), BF)
+    R.va[64:72, :] = jnp.where(row < 3, 1.0, 0.0).astype(BF)
+    R.va[72:128, :] = jnp.zeros((56, keys), BF)
+    qrow = lax.broadcasted_iota(jnp.int32, (8, span), 0)
+    hide = jnp.where((qrow < 5) & (own != (qrow - 1).astype(F32)), -BIG, 0.0)
+    hide = jnp.where(qrow == 5, -BIG, hide)
+    hide = jnp.where((qrow == 6) & (own == -1.0), -BIG, hide)
+    R.qa[64:72, :] = hide.astype(BF)
+    R.qa[72:128, :] = jnp.zeros((56, span), BF)
+    R.da[64:128, :] = jnp.zeros((64, span), BF)
+    R.P[toks + 32 : keys, :] = jnp.zeros((KEY_PAD - 32, WIDE), BF)
+
+
+def band_of(wave):
+    spread = jnp.broadcast_to(wave, (128, 512))
+    parts = [pltpu.roll(spread, 128 * n, 1, stride=1, stride_axis=0)[:, 0:128] for n in range(3)]
+    return jnp.concatenate(parts, axis=0)
+
+
+def unband(near):
+    empty = jnp.zeros((8, 128), F32)
+    total = None
+    for n in range(16):
+        part = jnp.concatenate(
+            [near[8 * n : 8 * n + 8], empty, near[256 + 8 * n : 264 + 8 * n], near[128 + 8 * n : 136 + 8 * n]], axis=1
+        )
+        if n:
+            part = pltpu.roll(part, 512 - 8 * n, 1)
+        total = part if total is None else total + part
+    row = lax.broadcasted_iota(jnp.int32, (8, 512), 0)
+    out = jnp.zeros((8, 512), F32)
+    for n in range(8):
+        out = out + jnp.where(row == n, total if n == 0 else pltpu.roll(total, 512 - n, 1), 0.0)
+    return jnp.sum(out, axis=0, keepdims=True)
+
+
+def layer_kernel(names, *refs):
+    R = Refs(**dict(zip(names, refs)))
+    place = Place()
+    links = Links(R.send_sems, R.recv_sems)
+    place.greet()
+    heads, span = R.QT.shape[0], R.QT.shape[2]
+    width = R.xin.shape[2]
+    group = heads // 4
+    kv_cols, q_cols = group * 128, group * HEAD_DIM
+    qkv_cols = kv_cols + q_cols
+    slots = R.xin.shape[0]
+    piece = R.xin.shape[1]
+
+    gather = [Gather(place, links, R.packed.at[n], R.W.at[n], R.local_sems.at[n]) for n in range(3)]
+    gather[0].start_z()
+    move_in = RowMove(place, links, R.hidden, R.xin)
+    gather[0].start_xy()
+    k_code = links.send(R.code.at[lax.rem(place.z, 2)], R.code_in, place.to_c)
+    at_mem = links.count
+    links.count += 4
+    mem_spot = R.KVT.at[pl.ds(group * place.z, group), :, 2 * span : 2 * span + KEY_PAD]
+    for r in (0, 1):
+        for c in (0, 1):
+            links.send_or_keep(
+                R.mem.at[r],
+                mem_spot,
+                {"c": c, "z": 2 * place.c + r},
+                (place.c == c) & (place.z == 2 * place.c + r),
+                at_mem + 2 * r + c,
+                at_mem + place.z,
+            )
+    gather[0].column()
+    gather[1].start_z()
+    gather[1].start_xy()
+
+    for s in range(slots):
+        move_in.wait(s)
+        _, hat = norm_parts(R.xin[s].astype(F32))
+        R.na[s * piece : (s + 1) * piece, :] = (hat * R.gains[0:1, :]).astype(BF)
+    links.arrived(R.code_in, k_code)
+    mask_rows(R, place)
+    gather[0].plane()
+    gather[1].column()
+    gather[0].corner()
+    gather[0].finish()
+
+    k_kv = []
+    for z in range(4):
+        low = dot(R.na[...], weights(R, 0, z, slice(0, qkv_cols))).astype(BF)
+        for j in range(group):
+            R.KVT[group * z + j, :, 0:span] = low[:, j * 128 : (j + 1) * 128].T
+        turned = (low[:, kv_cols:qkv_cols].astype(F32) * HEAD_DIM**-0.5).astype(BF).T
+        for j in range(group):
+            R.QT[group * z + j] = turned[j * HEAD_DIM : (j + 1) * HEAD_DIM, :]
+        block = pl.ds(group * z, group)
+        k_kv.append(links.send(R.KVT.at[block, :, 0:span], R.KVT.at[block, :, span : 2 * span], place.to_c))
+
+    gather[2].start_z()
+    gather[2].start_xy()
+    move_grad = RowMove(place, links, R.out_grad, R.gin)
+    gather[1].plane()
+
+    for z in range(4):
+        block = pl.ds(group * z, group)
+        links.arrived(R.KVT.at[block, :, span : 2 * span], k_kv[z])
+        links.arrived(R.KVT.at[block, :, 2 * span : 2 * span + KEY_PAD], at_mem + z)
+
+        @pl.loop(group * z, group * (z + 1))
+        def _(h):
+            fwd_head(R, h, place.c, R.table[15, h], R.table[31, h])
+
+        if z == 0:
+            gather[2].column()
+            gather[1].corner()
+        elif z == 1:
+            gather[2].plane()
+        elif z == 2:
+            gather[2].corner()
+    gather[1].finish()
+
+    for s in range(slots):
+        rows = slice(s * piece, (s + 1) * piece)
+        total = R.xin[s].astype(F32)
+        for z in range(4):
+            ctx = R.ctxT[group * z : group * (z + 1), :, rows].reshape(q_cols, piece).T
+            total = total + dot_t(ctx, weights(R, 0, z, slice(qkv_cols, width)))
+        R.mid[rows, :] = total
+        _, hat = norm_parts(total)
+        R.na[rows, :] = (hat * R.gains[1:2, :]).astype(BF)
+    R.nT[...] = R.na[...].T
+    gather[2].finish()
+    for s in range(slots):
+        move_grad.wait(s)
+        R.gT[:, s * piece : (s + 1) * piece] = R.gin[s].T
+
+    R.acc[...] = jnp.zeros_like(R.acc)
+    R.gacc[...] = jnp.zeros_like(R.gacc)
+
+    @pl.loop(0, 4)
+    def _(z):
+        for n in range(width // WIDE):
+            cols = slice(n * WIDE, (n + 1) * WIDE)
+            pre = dot(R.na[...], weights(R, 1, z, cols))
+            phi = 0.5 + 0.5 * lax.erf(pre * SQRT_HALF)
+            R.act[:, cols] = (pre * phi).astype(BF)
+            slope = phi + pre * (jnp.exp(-0.5 * pre * pre) * INV_SQRT_2PI)
+            back = dot(R.gin[...].reshape(span, width), weights(R, 2, z, cols))
+            R.gp[:, cols] = (back * slope).astype(BF)
+        R.acc[...] += dot_t(R.act[...], weights(R, 2, z, slice(0, width)))
+        R.gacc[...] += dot_t(R.gp[...], weights(R, 1, z, slice(0, width)))
+        R.G[2, z] = dot(R.gT[...], R.act[...]).astype(BF).reshape(4, 2, width // 8, width)
+        R.G[1, z] = dot(R.nT[...], R.gp[...]).astype(BF).reshape(4, 2, width // 8, width)
+
+    links.drain()
+    for peer in (place.to_x, place.to_y, place.to_c, place.to_z(1), place.to_z(2), place.to_z(3)):
+        pl.semaphore_signal(R.ready, inc=1, device_id=peer, device_id_type=MESH_ID)
+    gain_two = jnp.zeros((1, width), F32)
+    for s in range(slots):
+        rows = slice(s * piece, (s + 1) * piece)
+        mid = R.mid[rows, :]
+        R.ob[s] = (mid + R.acc[rows, :]).astype(BF)
+        inverse, hat = norm_parts(mid)
+        grad = R.gacc[rows, :]
+        gain_two = gain_two + jnp.sum(grad * hat, axis=0, keepdims=True)
+        scaled = grad * R.gains[1:2, :]
+        shift = hat * jnp.mean(scaled * hat, axis=-1, keepdims=True)
+        top = R.gin[s].astype(F32) + inverse * (scaled - shift)
+        R.mid[rows, :] = top
+        R.na[rows, :] = top.astype(BF)
+    R.small[...] = jnp.zeros_like(R.small)
+    R.small[1:2, :] = gain_two
+    move_out = RowMove(place, links, R.ob, R.output)
+    R.gT[...] = R.na[...].T
+    pl.semaphore_wait(R.ready, 6)
+    up_sum = Reduce(place, links, R.G.at[1], R.W.at[1])
+    down_sum = Reduce(place, links, R.G.at[2], R.W.at[2])
+    qkv_sum = Reduce(place, links, R.G.at[0], R.land)
+    for q in range(4):
+        up_sum.start(q)
+    for z in range(4):
+        ctx = R.ctxT[group * z : group * (z + 1)].reshape(q_cols, span)
+        part = dot_t(R.gT[...], ctx).astype(BF)
+        R.G[0, z, :, :, :, qkv_cols:] = part.reshape(4, 2, width // 8, q_cols)
+        turned = dot(R.na[...], weights(R, 0, z, slice(qkv_cols, width))).astype(BF).T
+        for j in range(group):
+            R.dOT[group * z + j] = turned[j * HEAD_DIM : (j + 1) * HEAD_DIM, :]
+    for s in range(slots):
+        _, hat = norm_parts(R.xin[s].astype(F32))
+        R.nT[:, s * piece : (s + 1) * piece] = (hat * R.gains[0:1, :]).astype(BF).T
+    R.gacc[...] = jnp.zeros_like(R.gacc)
+    for q in range(4):
+        up_sum.core(q)
+    for q in range(4):
+        down_sum.start(q)
+
+    def project_back(z):
+        links.arrived(R.kv_in.at[pl.ds(group * z, group)], k_back[z])
+        parts = []
+        for j in range(group):
+            whole = R.kv_own[group * (z % 2) + j] + R.kv_in[group * z + j].astype(F32)
+            parts.append(whole.astype(BF))
+        for j in range(group):
+            parts.append(R.dq[group * (z % 2) + j])
+        grads = jnp.concatenate(parts, axis=1)
+        made = dot(R.nT[...], grads).astype(BF)
+        R.G[0, z, :, :, :, 0:qkv_cols] = made.reshape(4, 2, width // 8, qkv_cols)
+        qkv_sum.start(z)
+        R.gacc[...] += dot_t(grads, weights(R, 0, z, slice(0, qkv_cols)))
+
+    k_back = []
+    for z in range(4):
+        block = pl.ds(group * z, group)
+
+        @pl.loop(0, group)
+        def _(j):
+            h = group * z + j
+            bwd_head(R, h, group * (z % 2) + j, place.c, R.table[15, h], R.table[31, h])
+
+        k_back.append(links.send(R.kv_out.at[block], R.kv_in.at[block], place.to_c))
+        if z > 0:
+            project_back(z - 1)
+        if z == 0:
+            for q in range(4):
+                up_sum.plane(q)
+            for q in range(4):
+                down_sum.core(q)
+        elif z == 1:
+            for q in range(4):
+                up_sum.column(q)
+            for q in range(4):
+                down_sum.plane(q)
+            qkv_sum.core(0)
+        elif z == 2:
+            up_sum.finish(R.gsum.at[1])
+            for q in range(4):
+                down_sum.column(q)
+            qkv_sum.plane(0)
+            qkv_sum.core(1)
+        else:
+            down_sum.finish(R.gsum.at[2])
+            qkv_sum.column(0)
+            qkv_sum.plane(1)
+            qkv_sum.core(2)
+    project_back(3)
+    gain_one = jnp.zeros((1, width), F32)
+    for s in range(slots):
+        rows = slice(s * piece, (s + 1) * piece)
+        inverse, hat = norm_parts(R.xin[s].astype(F32))
+        grad = R.gacc[rows, :]
+        gain_one = gain_one + jnp.sum(grad * hat, axis=0, keepdims=True)
+        scaled = grad * R.gains[0:1, :]
+        shift = hat * jnp.mean(scaled * hat, axis=-1, keepdims=True)
+        R.gin[s] = (R.mid[rows, :] + inverse * (scaled - shift)).astype(BF)
+    move_back = RowMove(place, links, R.gin, R.grad_in)
+    R.small[0:1, :] = gain_one
+
+    k = links.send(R.small, R.small_in.at[0], place.to_c)
+    qkv_sum.core(3)
+    qkv_sum.column(1)
+    qkv_sum.plane(2)
+    links.arrived(R.small_in.at[0], k)
+    R.small_in[0] = R.small_in[0] + R.small[...]
+    k = links.send(R.small_in.at[0], R.small_in.at[1], place.to_x)
+    qkv_sum.plane(3)
+    links.arrived(R.small_in.at[1], k)
+    R.small_in[1] = R.small_in[1] + R.small_in[0]
+    k = links.send(R.small_in.at[1], R.small_in.at[2], place.to_y)
+    qkv_sum.column(2)
+    links.arrived(R.small_in.at[2], k)
+    R.small_z[place.z] = R.small_in[2] + R.small_in[1]
+    own = R.small_z.at[place.z]
+    k_small = {k: links.send(own, own, place.to_z(k)) for k in (1, 2, 3)}
+    qkv_sum.column(3)
+    for k in (1, 2, 3):
+        links.arrived(R.small_z.at[place.from_z(k)], k_small[k])
+    R.small_sum[...] = (R.small_z[0] + R.small_z[1]) + (R.small_z[2] + R.small_z[3])
+    qkv_sum.finish(R.gsum.at[0])
+    for s in range(slots):
+        move_out.wait(s)
+        move_back.wait(s)
+    links.drain()
+
+
+def wave_buckets():
+    lane = np.arange(512)
+    apart = np.where(lane < 128, -lane - 128, 384 - lane)
+    far = np.abs(apart)
+    bucket = np.where(far < 8, far, 8 + sum((far >= bound).astype(np.int32) for bound in FAR_BOUNDS))
+    return bucket + np.where(apart > 0, 16, 0)
+
+
+def on_moved(
+    hidden_in,
+    out_grad,
+    seg_ids,
+    row_len,
+    slot_mask,
+    mem_keys,
+    mem_values,
+    w_qkv,
+    m_qkv,
+    v_qkv,
+    w_attn_out,
+    m_attn_out,
+    v_attn_out,
+    w_up,
+    m_up,
+    v_up,
+    w_down,
+    m_down,
+    v_down,
+    gains,
+    m_gains,
+    v_gains,
+    rel_table,
+    m_rel,
+    v_rel,
+):
+    rows, piece, width = hidden_in.shape
+    seq = seg_ids.shape[1]
+    span = seq // 2
+    slots = mem_keys.shape[1]
+    buckets, heads = rel_table.shape
+    group = heads // 4
+    shard = w_qkv.shape[1]
+    live = jnp.arange(seq, dtype=jnp.int32)[None, :] < row_len[:, None]
+    docs = jnp.where(live, seg_ids, -1)
+    on = jnp.where(jnp.repeat(slot_mask, 2, axis=1) > 0, 10, 11)
+    code = jnp.concatenate([docs, on, jnp.full((rows, KEY_PAD - slots), 11, jnp.int32)], axis=1)
+    code = jnp.broadcast_to(code[:, None, :].astype(F32), (rows, 8, seq + KEY_PAD))
+
+    def turned(mem):
+        return jnp.transpose(mem.reshape(rows, slots, group, HEAD_DIM), (0, 2, 3, 1))
+
+    mem = jnp.concatenate([turned(mem_keys), turned(mem_values)], axis=2)
+    mem = jnp.pad(mem, ((0, 0), (0, 0), (0, 0), (0, KEY_PAD - slots)))
+    w_low = w_qkv.astype(BF).reshape(3, shard, group, HEAD_DIM)
+    first = jnp.concatenate(
+        [
+            jnp.concatenate([w_low[1], w_low[2]], axis=2).reshape(shard, group * 128),
+            w_low[0].reshape(shard, group * HEAD_DIM),
+            w_attn_out.astype(BF).T,
+        ],
+        axis=1,
+    )
+    packed = jnp.stack([first, w_up.astype(BF), w_down.astype(BF).T])
+    hot = jnp.asarray(wave_buckets()[:, None] == np.arange(buckets)[None, :], F32)
+    wave = jnp.einsum("bh,mb->hm", rel_table, hot, precision=lax.Precision.HIGHEST)
+    wave = jnp.pad(wave, ((0, 16 - heads), (0, 0)))
+
+    any_space = pl.BlockSpec(memory_space=pl.ANY)
+    vmem = pl.BlockSpec(memory_space=pltpu.VMEM)
+    smem = pl.BlockSpec(memory_space=pltpu.SMEM)
+    keys = seq + KEY_PAD
+    scratch = {
+        "W": pltpu.VMEM((3, 4, 8, shard, width), BF),
+        "G": pltpu.VMEM((3, 4, 4, 2, shard, width), BF),
+        "land": pltpu.VMEM((4, 8, shard, width), BF),
+        "KVT": pltpu.VMEM((heads, 128, keys), BF),
+        "QT": pltpu.VMEM((heads, HEAD_DIM, span), BF),
+        "ctxT": pltpu.VMEM((heads, HEAD_DIM, span), BF),
+        "dOT": pltpu.VMEM((heads, HEAD_DIM, span), BF),
+        "lse": pltpu.VMEM((16, span), F32),
+        "xin": pltpu.VMEM((2, piece, width), BF),
+        "gin": pltpu.VMEM((2, piece, width), BF),
+        "ob": pltpu.VMEM((2, piece, width), BF),
+        "na": pltpu.VMEM((span, width), BF),
+        "nT": pltpu.VMEM((width, span), BF),
+        "gT": pltpu.VMEM((width, span), BF),
+        "act": pltpu.VMEM((span, width), BF),
+        "gp": pltpu.VMEM((span, width), BF),
+        "mid": pltpu.VMEM((span, width), F32),
+        "acc": pltpu.VMEM((span, width), F32),
+        "gacc": pltpu.VMEM((span, width), F32),
+        "kv_own": pltpu.VMEM((2 * group, span, 128), F32),
+        "kv_in": pltpu.VMEM((heads, span, 128), BF),
+        "kv_out": pltpu.VMEM((heads, span, 128), BF),
+        "dq": pltpu.VMEM((2 * group, span, HEAD_DIM), BF),
+        "S": pltpu.VMEM((seq + 32, WIDE), F32),
+        "P": pltpu.VMEM((keys, WIDE), BF),
+        "ka": pltpu.VMEM((128, keys), BF),
+        "va": pltpu.VMEM((128, keys), BF),
+        "Ka": pltpu.VMEM((keys, 128), BF),
+        "Va": pltpu.VMEM((keys, 128), BF),
+        "qa": pltpu.VMEM((128, span), BF),
+        "da": pltpu.VMEM((128, span), BF),
+        "band": pltpu.VMEM((384, 128), F32),
+        "code_in": pltpu.VMEM((8, keys), F32),
+        "small": pltpu.VMEM((24, width), F32),
+        "small_in": pltpu.VMEM((3, 24, width), F32),
+        "small_z": pltpu.VMEM((4, 24, width), F32),
+        "send_sems": pltpu.SemaphoreType.DMA((LINK_SEMS,)),
+        "recv_sems": pltpu.SemaphoreType.DMA((LINK_SEMS,)),
+        "local_sems": pltpu.SemaphoreType.DMA((3,)),
+        "ready": pltpu.SemaphoreType.REGULAR,
+    }
+    operands = {
+        "table": (rel_table, smem),
+        "code": (code, vmem),
+        "gains": (gains, vmem),
+        "wave": (wave, vmem),
+        "hidden": (hidden_in, any_space),
+        "out_grad": (out_grad, any_space),
+        "packed": (packed, any_space),
+        "mem": (mem, any_space),
+    }
+    results = {
+        "output": (jax.ShapeDtypeStruct(hidden_in.shape, BF), any_space),
+        "grad_in": (jax.ShapeDtypeStruct(hidden_in.shape, BF), any_space),
+        "gsum": (jax.ShapeDtypeStruct((3, shard, width), F32), vmem),
+        "small_sum": (jax.ShapeDtypeStruct((24, width), F32), vmem),
+    }
+    names = [*operands, *results, *scratch]
+    output, grad_input, gsum, small = pl.pallas_call(
+        functools.partial(layer_kernel, names),
+        out_shape=[shape for shape, _ in results.values()],
+        in_specs=[spec for _, spec in operands.values()],
+        out_specs=[spec for _, spec in results.values()],
+        scratch_shapes=list(scratch.values()),
+        compiler_params=pltpu.CompilerParams(
+            collective_id=0, has_side_effects=True, vmem_limit_bytes=VMEM_LIMIT
+        ),
+    )(*[array for array, _ in operands.values()])
+    gains_grad = small[0:2]
+    table_grad = jnp.einsum("hm,mb->bh", small[8 : 8 + heads, 0:512], hot, precision=lax.Precision.HIGHEST)
+    far = jnp.zeros((buckets, heads), F32).at[15].set(small[8 : 8 + heads, 512])
+    table_grad = table_grad + far.at[31].set(small[8 : 8 + heads, 513])
+    kv = gsum[0, :, 0 : group * 128].reshape(shard, group, 2, HEAD_DIM)
+    qkv_sum = jnp.stack(
+        [
+            gsum[0, :, group * 128 : group * 192],
+            kv[:, :, 0].reshape(shard, group * HEAD_DIM),
+            kv[:, :, 1].reshape(shard, group * HEAD_DIM),
+        ]
+    )
+    qkv = adamw(w_qkv, qkv_sum, m_qkv, v_qkv, MATRIX_RATE, WEIGHT_DECAY)
+    attn_out = adamw(
+        w_attn_out, gsum[0, :, group * 192 :].T, m_attn_out, v_attn_out, MATRIX_RATE, WEIGHT_DECAY
+    )
+    up = adamw(w_up, gsum[1], m_up, v_up, MATRIX_RATE, WEIGHT_DECAY)
+    down = adamw(w_down, gsum[2].T, m_down, v_down, MATRIX_RATE, WEIGHT_DECAY)
+    gain = adamw(gains, gains_grad, m_gains, v_gains, SMALL_RATE, 0.0)
+    rel = adamw(rel_table, table_grad, m_rel, v_rel, SMALL_RATE, 0.0)
+    out = [output, grad_input.astype(F32)]
+    for new, moment, second in (qkv, attn_out, up, down):
+        out += [new, moment, second, new.astype(BF)]
+    return (*out, *gain, *rel)
+
+
 def solution(mesh):
+    if dict(mesh.shape) == {"dp": 8, "mp": 4}:
+        mesh = Mesh(mesh.devices.reshape(2, 2, 2, 4), ("y", "x", "c", "z"))
+        return placed_on(mesh, on_moved, ("y", "x", "c"), "z")
+    return placed_on(mesh, on_device, "dp", "mp")
+
+
+def placed_on(mesh, body, dp, mp):
     placed = (
-        P("dp", "mp", None),
-        P("dp", "mp", None),
-        P("dp", None),
-        P("dp"),
-        P("dp", None),
-        P("dp", None, "mp"),
-        P("dp", None, "mp"),
-        P(None, "dp", "mp"),
-        P(None, "dp", "mp"),
-        P(None, "dp", "mp"),
-        P("mp", "dp"),
-        P("mp", "dp"),
-        P("mp", "dp"),
-        P("dp", "mp"),
-        P("dp", "mp"),
-        P("dp", "mp"),
-        P("mp", "dp"),
-        P("mp", "dp"),
-        P("mp", "dp"),
+        P(dp, mp, None),
+        P(dp, mp, None),
+        P(dp, None),
+        P(dp),
+        P(dp, None),
+        P(dp, None, mp),
+        P(dp, None, mp),
+        P(None, dp, mp),
+        P(None, dp, mp),
+        P(None, dp, mp),
+        P(mp, dp),
+        P(mp, dp),
+        P(mp, dp),
+        P(dp, mp),
+        P(dp, mp),
+        P(dp, mp),
+        P(mp, dp),
+        P(mp, dp),
+        P(mp, dp),
         P(),
         P(),
         P(),
@@ -393,28 +1292,28 @@
         P(),
     )
     return jax.shard_map(
-        on_device,
+        body,
         mesh=mesh,
         in_specs=placed,
         out_specs=(
-            P("dp", "mp", None),
-            P("dp", "mp", None),
-            P(None, "dp", "mp"),
-            P(None, "dp", "mp"),
-            P(None, "dp", "mp"),
-            P(None, "dp", "mp"),
-            P("mp", "dp"),
-            P("mp", "dp"),
-            P("mp", "dp"),
-            P("mp", "dp"),
-            P("dp", "mp"),
-            P("dp", "mp"),
-            P("dp", "mp"),
-            P("dp", "mp"),
-            P("mp", "dp"),
-            P("mp", "dp"),
-            P("mp", "dp"),
-            P("mp", "dp"),
+            P(dp, mp, None),
+            P(dp, mp, None),
+            P(None, dp, mp),
+            P(None, dp, mp),
+            P(None, dp, mp),
+            P(None, dp, mp),
+            P(mp, dp),
+            P(mp, dp),
+            P(mp, dp),
+            P(mp, dp),
+            P(dp, mp),
+            P(dp, mp),
+            P(dp, mp),
+            P(dp, mp),
+            P(mp, dp),
+            P(mp, dp),
+            P(mp, dp),
+            P(mp, dp),
             P(),
             P(),
             P(),

time: 1110 us -> 255 us (0.23)
  waiting for transfers between devices: 445 us -> 0 us
  other arithmetic: 323 us -> 10.4 us
  Pallas kernels: 0 us -> 223 us
  matrix products: 166 us -> 3.17 us
  blocking collectives: 66.7 us -> 0 us
  local copies, waits for them, and re-layouts: 75.1 us -> 12.9 us
  between operations: 16.6 us -> 1.35 us
    reduce_scatter x6 -> x0, waiting for transfers between devices: 264 us -> none  [the longest x1 110 us: on_device(): lax.psum_scatter(grad_normed_part, 'mp', scatter_dimension=1, tiled=True)]
    pallas_call x0 -> x1, Pallas kernels: none -> 223 us  [on_moved(): pl.pallas_call(functools.partial(layer_kernel, names), out_shape=[shape f...]
    all_gather x6 -> x0, waiting for transfers between devices: 180 us -> none  [the longest x1 61.4 us: on_device(): ffn_source = lax.all_gather(normed_two, 'mp', axis=1, tiled=True)]
    dot_general x60 -> x2, matrix products: 166 us -> 3.17 us  [the longest x1 1.88 us: on_moved(): jnp.einsum('hm,mb->bh', small[8:8 + heads, 0:512], hot, precision=lax.Pre...]
    eq x20 -> x0, other arithmetic: 97.7 us -> none  [the longest x16 95.1 us: on_device(): bucket_grid == bucket_number]
    reduce_sum x14 -> x0, other arithmetic: 81.4 us -> none  [the longest x2 67.8 us: on_device(): jnp.sum(jnp.where((bucket_grid == bucket_number)[None], bias_grad, 0.0),...]
    add x10 -> x0, other arithmetic: 76.6 us -> none  [the longest x1 54.1 us: on_device(): rel_bias + jnp.where((bucket_grid == bucket_number)[None], table_local[bu...]
    convert_element_type x14 -> x7, other arithmetic: 52.9 us -> 5.73 us  [the longest x4 4.45 us: on_moved(): out += [new, moment, second, new.astype(BF)]]
  transfers between devices with their start and end apart: 14 -> 0, of which waited for: 8 -> 0; matrix products, arithmetic and copies ran while one was open for 41% -> 0% of each run, Pallas kernels for 0% -> 0%
where the time goes in v1:
time: 255 us; the launch traced here: 251 us
  Pallas kernels  223 us (87%)
  local copies, waits for them, and re-layouts  12.9 us (5%)
  other arithmetic  10.4 us (4%)
  matrix products  3.17 us (1%)
    pallas_call x1, Pallas kernels, on_moved(): pl.pallas_call(functools.partial(layer_kernel, names), out_shape=[shape f...  223 us
    unnamed x37, local copies, waits for them, and re-layouts  7.89 us

profile of v1, /device:TPU:25, one launch (start us, length us, event | category | flops | bytes accessed | tf_op | source)
XLA Modules:
  0.0 250.6 jit_solution(9917855692656391886)
XLA Ops:
  0.7 0.8 compare_select_fusion.1
  1.5 0.8 compare_select_fusion
  2.5 1.4 copy.130.refs_0_
  3.9 1.3 convolution_bitcast_fusion
  6.4 1.0 copy.127
  7.5 0.9 copy.145
  8.4 0.9 copy.146
  9.3 0.7 fusion.5.refs_7_
  10.0 0.7 copy.134
  10.8 0.7 copy.135
  12.1 0.8 pad_maximum_fusion.refs_6_
  12.9 222.8 %shard_map.433 = (bf16[2,256,768]{2,1,0:T(8,128)(2,1)}, bf16[2,256,768]{2,1,0:T(8,128)(2,1)}, f32[3,96,768]{2,1,0:T(8,128)}, f32[24,768]{1,0:T(8,128)}) custom-call(f32[32,12]{1,0:T(8,128)} %copy.130.refs_0_, f32[2,8,1152]{2,1,0:T(8,128)} %broadcast_in_dim.31.refs_1_, f32[2,768]{1,0:T(2,128)} %refs_2_.1, f32[16,512]{1,0:T(8,128)} %pad.13.refs_3_, ...), custom_call_target="tpu_custom_call" | custom-call | tf_op jit(solution)/shard_map/pallas_call | solution.py:1223
  235.7 0.9 slice_bitcast_fusion.1
  236.7 1.9 multiply_subtract_fusion.4
  238.6 1.4 multiply_subtract_fusion.5
  240.0 1.1 fusion.16
  241.9 0.7 copy.140
  242.6 0.7 copy.141
  243.4 0.7 copy.142
  244.5 1.1 fusion.18
  245.6 1.1 fusion.12
  246.8 1.1 fusion.14
  248.0 1.3 convert_element_type.44
  249.3 0.9 copy.149
  (54 shorter events, 3.5 us)
Async XLA Ops:
  0.7 10.8 %copy-start = (f32[3,96,192]{2,1,0:T(8,128)S(1)}, f32[3,96,192]{2,1,0:T(8,128)}, u32[]{:S(2)}) copy-start(f32[3,96,192]{2,1,0:T(8,128)} %param.37) | copy-start | bytes 663556
  0.7 10.1 %copy-start.13 = (f32[192,96]{1,0:T(8,128)S(1)}, f32[192,96]{1,0:T(8,128)}, u32[]{:S(2)}) copy-start(f32[192,96]{1,0:T(8,128)} %param.42) | copy-start | bytes 221188
  0.7 9.3 %copy-start.12 = (f32[192,96]{1,0:T(8,128)S(1)}, f32[192,96]{1,0:T(8,128)}, u32[]{:S(2)}) copy-start(f32[192,96]{1,0:T(8,128)} %param.41) | copy-start | bytes 221188
  5.8 6.2 %copy-start.2 = (f32[96,768]{1,0:T(8,128)S(1)}, f32[96,768]{1,0:T(8,128)}, u32[]{:S(2)}) copy-start(f32[96,768]{1,0:T(8,128)} %param.43) | copy-start | bytes 884740
  7.4 4.6 %copy-start.1 = (f32[768,96]{0,1:T(8,128)S(1)}, f32[768,96]{0,1:T(8,128)}, u32[]{:S(2)}) copy-start(f32[768,96]{0,1:T(8,128)} %param.46) | copy-start | bytes 884740
  235.7 8.4 %copy-start.3 = (f32[3,96,768]{2,1,0:T(8,128)S(1)}, f32[3,96,768]{2,1,0:T(8,128)}, u32[]{:S(2)}) copy-start(f32[3,96,768]{2,1,0:T(8,128)} %get-tuple-element.54) | copy-start | bytes 2654212
  238.6 5.9 %copy-start.6 = (f32[3,96,192]{2,1,0:T(8,128)S(1)}, f32[3,96,192]{2,1,0:T(8,128)}, u32[]{:S(2)}) copy-start(f32[3,96,192]{2,1,0:T(8,128)} %param.38) | copy-start | bytes 663556
  238.6 5.9 %copy-start.7 = (f32[3,96,192]{2,1,0:T(8,128)S(1)}, f32[3,96,192]{2,1,0:T(8,128)}, u32[]{:S(2)}) copy-start(f32[3,96,192]{2,1,0:T(8,128)} %param.39) | copy-start | bytes 663556
  244.3 1.4 copy-start.8
  244.3 1.4 copy-start.9
  245.6 1.1 copy-start.10
  245.6 1.2 copy-start.11
  246.7 1.3 copy-start.5
  247.9 1.4 copy-start.4
